TPU v7x, 256 devices: a whole 4x4x8 slice. The times are simulated.
256 devices in a mesh: dp: 16 (over z, core), expert: 4 (over y), blk: 4 (over x).
Axes of the slice: x: 4, y: 4, z: 8, core: 2. Of those that a mesh axis runs over, the one named last changes fastest.
Arguments:
- tokens: bfloat16 [2048, 6144], P('dp', 'blk'), may hold values from -6 to 6
- expert_ids: int32 [2048, 2], P('dp'), may hold values from 0 to 7, all different within a row; in each aligned block of 128 rows (0 to 127, 128 to 255, ...) at most 48 rows name the same one
- route_weights: float32 [2048, 2], P('dp'), may hold values from 0.1 to 1
- gate_weight: bfloat16 [8, 6144, 8192], P('expert', 'blk', 'dp'), may hold values from -0.078125 to 0.078125
- up_weight: bfloat16 [8, 6144, 8192], P('expert', 'blk', 'dp'), may hold values from -0.078125 to 0.078125
- down_weight: bfloat16 [8, 8192, 6144], P('expert', 'dp', 'blk'), may hold values from -0.0625 to 0.0625
Outputs:
- mixed: bfloat16 [2048, 6144], P('dp', 'blk')
Inputs may be any that keep to these rules, and one draw needn't show every extreme that they name: `expert_ids`: each row names 2 different experts. Among the 128 rows of one data shard no expert is named more than 48 times, and in every draw some expert is named exactly 48 times in some shard.
All inputs are finite; a program needn't handle non-finite values.
Results may differ from a plain program's by a relative error of at most 0.0051.
Values may be sent and summed in bfloat16 or wider, within the bound.
A program may use at most 64 MiB of HBM per device.

v0:
```python
import jax
import jax.numpy as jnp
from jax import lax
from jax.sharding import PartitionSpec as P

EXPERTS = 8
CAP = 48


def local(tokens, expert_ids, route_weights, gate_weight, up_weight, down_weight):
    local_count = gate_weight.shape[0]
    token_count = tokens.shape[0]
    top_count = expert_ids.shape[1]
    group_index = lax.axis_index("expert")
    flat_ids = expert_ids.reshape(-1)
    one_hot = (flat_ids[:, None] == jnp.arange(EXPERTS, dtype=jnp.int32)[None, :]).astype(jnp.int32)
    before = jnp.cumsum(one_hot, axis=0) - one_hot
    position = jnp.sum(before * one_hot, axis=1)
    local_ids = flat_ids - group_index * local_count
    is_mine = local_ids[:, None] == jnp.arange(local_count, dtype=jnp.int32)[None, :]
    in_slot = position[:, None] == jnp.arange(CAP, dtype=jnp.int32)[None, :]
    slot_hit = (is_mine[:, :, None] & in_slot[:, None, :]).reshape(
        token_count, top_count, local_count, CAP
    )
    dispatch = jnp.any(slot_hit, axis=1).astype(jnp.bfloat16)
    combine = jnp.sum(slot_hit.astype(jnp.float32) * route_weights[:, :, None, None], axis=1)
    picked = jnp.einsum("tec,tf->ecf", dispatch, tokens, preferred_element_type=jnp.float32).astype(
        jnp.bfloat16
    )
    shard_rows = lax.all_gather(picked, "dp", axis=1, tiled=True)
    gate_part = jnp.einsum(
        "enf,efh->enh", shard_rows, gate_weight, preferred_element_type=jnp.float32
    )
    up_part = jnp.einsum("enf,efh->enh", shard_rows, up_weight, preferred_element_type=jnp.float32)
    partial_value = jnp.stack([gate_part, up_part])
    summed = lax.psum(partial_value, "blk")
    hidden = (jax.nn.silu(summed[0]) * summed[1]).astype(jnp.bfloat16)
    expert_out = lax.psum_scatter(
        jnp.einsum("enh,ehd->ned", hidden, down_weight, preferred_element_type=jnp.float32),
        "dp",
        scatter_dimension=0,
        tiled=True,
    )
    mixed_part = jnp.einsum("tec,ced->td", combine, expert_out, precision=lax.Precision.HIGHEST)
    mixed = lax.psum(mixed_part, "expert")
    return mixed.astype(jnp.bfloat16)


def solution(mesh):
    placed = (
        P("dp", "blk"),
        P("dp", None),
        P("dp", None),
        P("expert", "blk", "dp"),
        P("expert", "blk", "dp"),
        P("expert", "dp", "blk"),
    )
    return jax.shard_map(
        local, mesh=mesh, in_specs=placed, out_specs=P("dp", "blk"), check_vma=False
    )
```

profile of v0, /device:TPU:2, one launch (start us, length us, event | category | flops | bytes accessed | tf_op | source)
XLA Modules:
  0.0 316.2 jit_solution(18314517861227424447)
XLA Ops:
  6.5 0.0 copy-start
  6.5 0.0 all-gather.2.cloned.1.call-start
  6.5 0.9 copy.13
  7.5 0.1 eq.65
  7.6 0.1 reshape.70
  7.8 0.6 reduce-window.6
  8.4 0.2 slice_reduce_fusion
  8.6 0.1 fusion.7
  8.7 0.1 eq.69
  8.9 0.1 copy.15
  9.0 0.7 broadcast_subtract_fusion
  9.7 1.9 convolution_convert_fusion
  11.6 0.0 all-gather.2.cloned.1.call-update
  11.7 0.0 all-reduce.3.cloned.1.call-start
  11.7 45.8 %all-gather.2.cloned.1.call-done = bf16[2,768,1536]{2,1,0:T(8,128)(2,1)} async-done(((bf16[2,48,1536]{2,1,0:T(8,128)(2,1)}), bf16[2,768,1536]{2,1,0:T(8,128)(2,1)}) %all-gather.2.cloned.1.call-update) | async-done | bytes 4718608 | tf_op jit(solution)/shard_map/all_gather | solution.py:30
  57.5 0.0 copy-start.2
  57.5 0.0 copy-start.3
  57.5 5.5 %convolution_bitcast_fusion.2 = f32[1,2,768,512]{3,2,1,0:T(8,128)S(1)} fusion(bf16[2,768,1536]{2,1,0:T(8,128)(2,1)} %all-gather.2.cloned.1.call-done, bf16[2,1536,512]{2,1,0:T(8,128)(2,1)} %param.10), kind=kOutput, calls=%fused_computation.8 | convolution fusion | flops 2415919104 | bytes 11010048 | tf_op jit(solution)/shard_map/enf,efh->enh/dot_general | solution.py:34
  63.0 0.0 copy-done.2
  63.0 0.1 copy-done.3
  63.1 2.6 convolution_bitcast_fusion.3
  65.7 3.4 %pad_maximum_fusion = f32[2,2,768,512]{3,2,1,0:T(8,128)} fusion(f32[1,2,768,512]{3,2,1,0:T(8,128)S(1)} %convolution_bitcast_fusion.2, f32[1,2,768,512]{3,2,1,0:T(8,128)S(1)} %convolution_bitcast_fusion.3), kind=kLoop, calls=%fused_computation | loop fusion | flops 1572864 | bytes 12582912 | tf_op jit(solution)/shard_map/stack | solution.py:35
  69.1 0.0 all-reduce.3.cloned.1.call-update
  69.1 0.0 reduce-scatter.2.cloned.1.call-start
  69.1 129.7 %all-reduce.3.cloned.1.call-done = f32[2,2,768,512]{3,2,1,0:T(8,128)} async-done(((f32[2,2,768,512]{3,2,1,0:T(8,128)}), f32[2,2,768,512]{3,2,1,0:T(8,128)}) %all-reduce.3.cloned.1.call-update) | async-done | bytes 6291472 | tf_op jit(solution)/shard_map/psum | solution.py:36
  198.9 0.0 copy-done
  198.9 8.0 %convolution_bitcast_fusion = f32[768,2,1536]{2,0,1:T(8,128)} fusion(bf16[2,512,1536]{2,1,0:T(8,128)(2,1)S(1)} %copy-done, f32[2,2,768,512]{3,2,1,0:T(8,128)} %all-reduce.3.cloned.1.call-done), kind=kOutput, calls=%fused_computation.1 | convolution fusion | flops 2420637696 | bytes 18874368 | tf_op jit(solution)/shard_map/enh,ehd->ned/dot_general | solution.py:39
  206.9 0.0 copy-start.1
  206.9 0.0 reduce-scatter.2.cloned.1.call-update
  206.9 0.7 copy-done.1
  207.6 73.1 %reduce-scatter.2.cloned.1.call-done = f32[48,2,1536]{2,0,1:T(8,128)} async-done(((f32[768,2,1536]{2,0,1:T(8,128)}), f32[48,2,1536]{2,0,1:T(8,128)}) %reduce-scatter.2.cloned.1.call-update) | async-done | bytes 589840 | tf_op jit(solution)/shard_map/reduce_scatter | solution.py:38
  280.7 2.8 convolution_bitcast_fusion.1
  283.5 26.3 %all-reduce.4 = bf16[128,1536]{1,0:T(8,128)(2,1)} all-reduce(f32[128,1536]{1,0:T(8,128)} %convolution_bitcast_fusion.1), channel_id=1, replica_groups=mesh['dp'=16,'expert'=4,'blk'=4] {'expert'}, use_global_device_ids=true, to_apply=%region_7.8 | all-reduce | flops 196608 | bytes 1179648 | tf_op jit(solution)/shard_map/psum | solution.py:45
  (7 shorter events, 0.1 us)
Async XLA Ops:
  6.5 192.3 %copy-start = (bf16[2,512,1536]{2,1,0:T(8,128)(2,1)S(1)}, bf16[2,512,1536]{2,1,0:T(8,128)(2,1)}, u32[]{:S(2)}) copy-start(bf16[2,512,1536]{2,1,0:T(8,128)(2,1)} %param.11) | copy-start | bytes 9437188
  6.5 50.9 %all-gather.2.cloned.1.call-start = ((), (), s32[]{:S(2)}) async-start(), calls=%async_computation.1 | async-start | bytes 5013504 | tf_op jit(solution)/shard_map/all_gather | solution.py:30
  11.7 187.2 %all-reduce.3.cloned.1.call-start = ((), (), s32[]{:S(2)}) async-start(), calls=%async_computation.2 | async-start | bytes 12582912 | tf_op jit(solution)/shard_map/psum | solution.py:36
  57.5 5.6 %copy-start.2 = (bf16[2,768,1536]{2,1,0:T(8,128)(2,1)S(1)}, bf16[2,768,1536]{2,1,0:T(8,128)(2,1)}, u32[]{:S(2)}) copy-start(bf16[2,768,1536]{2,1,0:T(8,128)(2,1)} %all-gather.2.cloned.1.call-done) | copy-start | bytes 14155780
  57.5 5.6 %copy-start.3 = (bf16[2,1536,512]{2,1,0:T(8,128)(2,1)S(1)}, bf16[2,1536,512]{2,1,0:T(8,128)(2,1)}, u32[]{:S(2)}) copy-start(bf16[2,1536,512]{2,1,0:T(8,128)(2,1)} %param.9) | copy-start | bytes 9437188
  69.1 211.6 %reduce-scatter.2.cloned.1.call-start = ((), (), s32[]{:S(2)}) async-start(), calls=%async_computation.3 | async-start | bytes 10027008 | tf_op jit(solution)/shard_map/reduce_scatter | solution.py:38
  206.9 0.7 copy-start.1
Sparse Core Ops, SparseCore 0:
  11.8 45.6 all-gather.1
  69.2 129.6 all-reduce.2
  207.0 73.5 reduce-scatter.1
where the time goes:
time: 316 us
  waiting for transfers between devices  249 us (79%)
  blocking collectives  26.3 us (8%)
  matrix products  20.9 us (7%)
  between operations  13.2 us (4%)
  other arithmetic  4.85 us (2%)
    psum x1, waiting for transfers between devices, local(): summed = lax.psum(partial_value, 'blk')  130 us
    reduce_scatter x1, waiting for transfers between devices, local(): lax.psum_scatter(jnp.einsum('enh,ehd->ned', hidden, down_weight, preferre...  73.1 us
    all_gather x1, waiting for transfers between devices, local(): shard_rows = lax.all_gather(picked, 'dp', axis=1, tiled=True)  45.8 us
    psum x1, blocking collectives, local(): mixed = lax.psum(mixed_part, 'expert')  26.3 us
    dot_general x1, matrix products, local(): jnp.einsum('enh,ehd->ned', hidden, down_weight, preferred_element_type=jn...  8.03 us
  transfers between devices with their start and end apart: 3, of which 3 were waited for; matrix products, arithmetic and copies ran while one was open for 0% of the time, Pallas kernels for 0%

commit v1 on v0

--- a/solution.py
+++ b/solution.py
@@ -33,7 +33,9 @@
     )
     up_part = jnp.einsum("enf,efh->enh", shard_rows, up_weight, preferred_element_type=jnp.float32)
     partial_value = jnp.stack([gate_part, up_part])
-    summed = lax.psum(partial_value, "blk")
+    summed = partial_value
+    for hop in (1, 2):
+        summed = summed + lax.ppermute(summed, "blk", [(dev, dev ^ hop) for dev in range(4)])
     hidden = (jax.nn.silu(summed[0]) * summed[1]).astype(jnp.bfloat16)
     expert_out = lax.psum_scatter(
         jnp.einsum("enh,ehd->ned", hidden, down_weight, preferred_element_type=jnp.float32),

time: 316 us -> 474 us (1.50)
  waiting for transfers between devices: 249 us -> 390 us
  other arithmetic: 4.85 us -> 17.5 us
    ppermute x0 -> x2, waiting for transfers between devices: none -> 274 us  [local(): lax.ppermute(summed, 'blk', [(dev, dev ^ hop) for dev in range(4)])]
    psum x1 -> x0, waiting for transfers between devices: 130 us -> none  [local(): summed = lax.psum(partial_value, 'blk')]
    add x0 -> x2, other arithmetic: none -> 15 us  [local(): summed + lax.ppermute(summed, 'blk', [(dev, dev ^ hop) for dev in range(4)])]
  transfers between devices with their start and end apart: 3 -> 4, of which waited for: 3 -> 4; matrix products, arithmetic and copies ran while one was open for 0% -> 0% of each run, Pallas kernels for 0% -> 0%
where the time goes in v1:
time: 474 us
  waiting for transfers between devices  390 us (82%)
  blocking collectives  26.5 us (6%)
  matrix products  20.9 us (4%)
  other arithmetic  17.5 us (4%)
  between operations  13.5 us (3%)
    ppermute x2, waiting for transfers between devices, local(): lax.ppermute(summed, 'blk', [(dev, dev ^ hop) for dev in range(4)])  274 us
    reduce_scatter x1, waiting for transfers between devices, local(): lax.psum_scatter(jnp.einsum('enh,ehd->ned', hidden, down_weight, preferre...  70.7 us
    all_gather x1, waiting for transfers between devices, local(): shard_rows = lax.all_gather(picked, 'dp', axis=1, tiled=True)  45.8 us
    psum x1, blocking collectives, local(): mixed = lax.psum(mixed_part, 'expert')  26.5 us
    add x2, other arithmetic, local(): summed + lax.ppermute(summed, 'blk', [(dev, dev ^ hop) for dev in range(4)])  15 us
  transfers between devices with their start and end apart: 4, of which 4 were waited for; matrix products, arithmetic and copies ran while one was open for 0% of the time, Pallas kernels for 0%

profile of v1, /device:TPU:2, one launch (start us, length us, event | category | flops | bytes accessed | tf_op | source)
XLA Modules:
  0.0 473.7 jit_solution(515828243712616681)
XLA Ops:
  6.5 0.0 copy-start
  6.5 0.0 all-gather.2.cloned.1.call-start
  6.5 0.9 copy.13
  7.5 0.1 eq.65
  7.6 0.1 reshape.70
  7.8 0.6 reduce-window.6
  8.4 0.2 slice_reduce_fusion
  8.6 0.1 fusion.7
  8.7 0.1 eq.69
  8.9 0.1 copy.15
  9.0 0.7 broadcast_subtract_fusion
  9.7 1.9 convolution_convert_fusion
  11.6 0.0 all-gather.2.cloned.1.call-update
  11.7 0.0 reduce-scatter.2.cloned.1.call-start
  11.7 45.8 %all-gather.2.cloned.1.call-done = bf16[2,768,1536]{2,1,0:T(8,128)(2,1)} async-done(((bf16[2,48,1536]{2,1,0:T(8,128)(2,1)}), bf16[2,768,1536]{2,1,0:T(8,128)(2,1)}) %all-gather.2.cloned.1.call-update) | async-done | bytes 4718608 | tf_op jit(solution)/shard_map/all_gather | solution.py:30
  57.5 0.0 copy-start.4
  57.5 0.0 copy-start.5
  57.5 5.5 %convolution_bitcast_fusion.2 = f32[1,2,768,512]{3,2,1,0:T(8,128)S(1)} fusion(bf16[2,768,1536]{2,1,0:T(8,128)(2,1)} %all-gather.2.cloned.1.call-done, bf16[2,1536,512]{2,1,0:T(8,128)(2,1)} %param.10), kind=kOutput, calls=%fused_computation.8 | convolution fusion | flops 2415919104 | bytes 11010048 | tf_op jit(solution)/shard_map/enf,efh->enh/dot_general | solution.py:34
  63.0 0.0 copy-done.4
  63.0 0.1 copy-done.5
  63.1 2.6 convolution_bitcast_fusion.3
  65.7 0.0 copy-start.1
  65.7 1.0 pad_maximum_fusion
  66.7 0.7 collective-permute-start
  67.5 137.0 %collective-permute-done = f32[2,2,768,512]{3,2,1,0:T(8,128)S(1)} collective-permute-done((f32[2,2,768,512]{3,2,1,0:T(8,128)S(1)}, f32[2,2,768,512]{3,2,1,0:T(8,128)S(1)}, u32[]{:S(2)}, u32[]{:S(2)}) %collective-permute-start) | collective-permute-done | bytes 6291488 | tf_op jit(solution)/shard_map/ppermute | solution.py:38
  204.5 0.0 copy-done.1
  204.5 0.0 copy-start.2
  204.5 4.5 fusion.10
  209.0 0.0 copy-done.2
  209.0 2.1 collective-permute-start.1
  211.1 136.6 %collective-permute-done.1 = f32[2,2,768,512]{3,2,1,0:T(8,128)} collective-permute-done((f32[2,2,768,512]{3,2,1,0:T(8,128)}, f32[2,2,768,512]{3,2,1,0:T(8,128)}, u32[]{:S(2)}, u32[]{:S(2)}) %collective-permute-start.1) | collective-permute-done | bytes 6291488 | tf_op jit(solution)/shard_map/ppermute | solution.py:38
  347.7 10.5 %fusion.19 = f32[2,2,768,512]{3,2,1,0:T(8,128)} fusion(f32[2,2,768,512]{3,2,1,0:T(8,128)} %collective-permute-done.1, f32[2,2,768,512]{3,2,1,0:T(8,128)} %copy-done.2, f32[1,2,768,512]{3,2,1,0:T(8,128)S(1)} %convolution_bitcast_fusion.2, f32[1,2,768,512]{3,2,1,0:T(8,128)} %copy-done.1), kind=kLoop, calls=%fused_computation.27 | loop fusion | flops 4718592 | bytes 25165824 | tf_op jit(solution)/shard_map/add | solution.py:38
  358.2 0.0 copy-done
  358.2 8.0 %convolution_bitcast_fusion = f32[768,2,1536]{2,0,1:T(8,128)} fusion(bf16[2,512,1536]{2,1,0:T(8,128)(2,1)S(1)} %copy-done, f32[2,2,768,512]{3,2,1,0:T(8,128)} %fusion.19), kind=kOutput, calls=%fused_computation.1 | convolution fusion | flops 2420637696 | bytes 18874368 | tf_op jit(solution)/shard_map/enh,ehd->ned/dot_general | solution.py:41
  366.2 0.0 copy-start.3
  366.2 0.0 reduce-scatter.2.cloned.1.call-update
  366.2 0.7 copy-done.3
  366.9 70.7 %reduce-scatter.2.cloned.1.call-done = f32[48,2,1536]{2,0,1:T(8,128)} async-done(((f32[768,2,1536]{2,0,1:T(8,128)}), f32[48,2,1536]{2,0,1:T(8,128)}) %reduce-scatter.2.cloned.1.call-update) | async-done | bytes 589840 | tf_op jit(solution)/shard_map/reduce_scatter | solution.py:40
  437.6 2.8 convolution_bitcast_fusion.1
  440.4 26.5 %all-reduce.1 = bf16[128,1536]{1,0:T(8,128)(2,1)} all-reduce(f32[128,1536]{1,0:T(8,128)} %convolution_bitcast_fusion.1), channel_id=1, replica_groups=mesh['dp'=16,'expert'=4,'blk'=4] {'expert'}, use_global_device_ids=true, to_apply=%region_6.7 | all-reduce | flops 196608 | bytes 1179648 | tf_op jit(solution)/shard_map/psum | solution.py:47
  (7 shorter events, 0.1 us)
Async XLA Ops:
  6.5 351.6 %copy-start = (bf16[2,512,1536]{2,1,0:T(8,128)(2,1)S(1)}, bf16[2,512,1536]{2,1,0:T(8,128)(2,1)}, u32[]{:S(2)}) copy-start(bf16[2,512,1536]{2,1,0:T(8,128)(2,1)} %param.11) | copy-start | bytes 9437188
  6.5 50.9 %all-gather.2.cloned.1.call-start = ((), (), s32[]{:S(2)}) async-start(), calls=%async_computation.1 | async-start | bytes 5013504 | tf_op jit(solution)/shard_map/all_gather | solution.py:30
  11.7 425.9 %reduce-scatter.2.cloned.1.call-start = ((), (), s32[]{:S(2)}) async-start(), calls=%async_computation.2 | async-start | bytes 10027008 | tf_op jit(solution)/shard_map/reduce_scatter | solution.py:40
  57.5 5.6 %copy-start.4 = (bf16[2,768,1536]{2,1,0:T(8,128)(2,1)S(1)}, bf16[2,768,1536]{2,1,0:T(8,128)(2,1)}, u32[]{:S(2)}) copy-start(bf16[2,768,1536]{2,1,0:T(8,128)(2,1)} %all-gather.2.cloned.1.call-done) | copy-start | bytes 14155780
  57.5 5.6 %copy-start.5 = (bf16[2,1536,512]{2,1,0:T(8,128)(2,1)S(1)}, bf16[2,1536,512]{2,1,0:T(8,128)(2,1)}, u32[]{:S(2)}) copy-start(bf16[2,1536,512]{2,1,0:T(8,128)(2,1)} %param.9) | copy-start | bytes 9437188
  65.7 138.8 %copy-start.1 = (f32[1,2,768,512]{3,2,1,0:T(8,128)}, f32[1,2,768,512]{3,2,1,0:T(8,128)S(1)}, u32[]{:S(2)}) copy-start(f32[1,2,768,512]{3,2,1,0:T(8,128)S(1)} %convolution_bitcast_fusion.3) | copy-start | bytes 9437188
  66.7 137.8 %collective-permute-start = (f32[2,2,768,512]{3,2,1,0:T(8,128)S(1)}, f32[2,2,768,512]{3,2,1,0:T(8,128)S(1)}, u32[]{:S(2)}, u32[]{:S(2)}) collective-permute-start(f32[2,2,768,512]{3,2,1,0:T(8,128)S(1)} %pad_maximum_fusion), channel_id=1, source_target_pairs={{0,1},{1,0},{2,3},{3,2},{4,5},{5,4},{6,7},{7,6},{8,9},{9,8},{10,11... | collective-permute-start | bytes 18874376 | tf_op jit(solution)/shard_map/ppermute | solution.py:38
  204.5 4.5 copy-start.2
  209.0 138.7 %collective-permute-start.1 = (f32[2,2,768,512]{3,2,1,0:T(8,128)}, f32[2,2,768,512]{3,2,1,0:T(8,128)}, u32[]{:S(2)}, u32[]{:S(2)}) collective-permute-start(f32[2,2,768,512]{3,2,1,0:T(8,128)} %fusion.10), channel_id=1, source_target_pairs={{0,2},{1,3},{2,0},{3,1},{4,6},{5,7},{6,4},{7,5},{8,10},{9,11},{10,... | collective-permute-start | bytes 18874376 | tf_op jit(solution)/shard_map/ppermute | solution.py:38
  366.2 0.7 copy-start.3
Sparse Core Ops, SparseCore 0:
  11.8 45.6 all-gather.1
  366.3 71.2 reduce-scatter.1
